TPU v7x, 32 devices: a whole 2x2x4 slice. The times are simulated.
32 devices in a mesh: dp: 1, mp: 32 (over z, y, x, core).
Axes of the slice: x: 2, y: 2, z: 4, core: 2. Of those that a mesh axis runs over, the one named last changes fastest.
Arguments:
- grads: bfloat16 [1, 16, 32, 256, 256], P('dp', None, 'mp'), may hold values from -18 to 18
- layer_map: int32 [512], replicated, may hold values from 0 to 31, never falling along the last dimension, each value on 1 to 32 neighbouring positions
Outputs:
- roots: float32 [16, 32, 256, 256], P(None, 'mp', 'dp')
Inputs may be any that keep to these rules, and one draw needn't show every extreme that they name: `layer_map`: layer numbers never fall along b; every layer 0 to 31 holds 1 to 32 blocks.
All inputs are finite; a program needn't handle non-finite values.
Results may differ from a plain program's by a relative error of at most 0.0003.
Values sent between devices are 32-bit elements; how exact they have to be, the bound alone decides.
A program may use at most 64 MiB of HBM per device.

v0:
```python
import functools

import jax
import jax.numpy as jnp
from jax import lax
from jax.experimental import pallas as pl
from jax.experimental.pallas import tpu as pltpu
from jax.sharding import PartitionSpec as P

ITERS = 8


def newton_root(stats, ridge, live):
    order = stats.shape[-1]
    identity = jnp.eye(order, dtype=jnp.float32)
    damped = jnp.where(live[:, None, None], stats + ridge[:, None, None] * identity, identity)
    frobenius = jnp.sqrt(jnp.sum(damped * damped, axis=(1, 2)))
    scaled = 2.5 / frobenius
    current = (scaled**0.25)[:, None, None] * identity
    coupled = scaled[:, None, None] * damped
    for _ in range(ITERS):
        factor = 1.25 * identity - 0.25 * coupled
        current = jnp.einsum("sij,sjk->sik", current, factor, precision=lax.Precision.HIGHEST)
        square = jnp.einsum("sij,sjk->sik", factor, factor, precision=lax.Precision.HIGHEST)
        fourth = jnp.einsum("sij,sjk->sik", square, square, precision=lax.Precision.HIGHEST)
        coupled = jnp.einsum("sij,sjk->sik", fourth, coupled, precision=lax.Precision.HIGHEST)
    return current


def local_split(grads, layer_map):
    gradient = grads[0, :, 0]
    blocks_here, order, columns = gradient.shape
    replicas = lax.axis_size("dp")
    holders = lax.axis_size("mp")
    band = order // replicas
    replica = lax.axis_index("dp")
    holder = lax.axis_index("mp")
    partial_value = jnp.einsum(
        "bic,bjc->bij", gradient, gradient, preferred_element_type=jnp.float32
    ) * (1.0 / (replicas * columns))
    summed = lax.psum(partial_value, "dp")
    mine = lax.dynamic_slice_in_dim(summed, replica * band, band, 1)
    layer_grid = layer_map.reshape(blocks_here, holders)
    my_layers = lax.dynamic_slice_in_dim(layer_grid, holder, 1, 1)[:, 0]
    layer_ids = jnp.arange(holders, dtype=jnp.int32)
    local_onehot = (my_layers[:, None] == layer_ids[None, :]).astype(jnp.float32)
    all_counts = jnp.sum((layer_map[:, None] == layer_ids[None, :]).astype(jnp.int32), axis=0)
    diag_rows = lax.dynamic_slice_in_dim(mine, replica * band, band, 2)
    diag_part = jnp.trace(diag_rows, axis1=1, axis2=2)
    layer_part = jnp.dot(diag_part, local_onehot, precision=lax.Precision.HIGHEST)
    layer_total = lax.psum(layer_part, ("dp", "mp"))
    layer_ridge = 0.1 * layer_total / (all_counts.astype(jnp.float32) * order)
    spread = -(-blocks_here // replicas)
    extra = replicas * spread - blocks_here
    stacked = lax.all_to_all(mine, "dp", split_axis=0, concat_axis=1, tiled=True)
    block_ridge = jnp.pad(
        jnp.dot(local_onehot, layer_ridge, precision=lax.Precision.HIGHEST), (0, extra)
    )
    slot_ridge = lax.dynamic_slice_in_dim(block_ridge, replica * spread, spread, 0)
    slot_index = replica * spread + jnp.arange(spread, dtype=jnp.int32)
    solved = newton_root(stacked, slot_ridge, slot_index < blocks_here)
    returned = lax.all_to_all(solved, "dp", split_axis=1, concat_axis=0, tiled=True)
    result = returned[:blocks_here]
    return result.reshape(blocks_here, 1, band, order)


LANES = 128
TOGETHER = 2
RECENTRE = (2, 4, 6)


def trace_exchange(holders, grad_ref, total_ref, slots, send_sem, recv_sem):
    me = lax.axis_index("mp")
    peers = [lax.rem(me + step, holders) for step in range(1, holders)]
    barrier = pltpu.get_barrier_semaphore()
    for peer in peers:
        pl.semaphore_signal(
            barrier, inc=1, device_id={"mp": peer}, device_id_type=pl.DeviceIdType.MESH
        )
    blocks_here, _, columns = grad_ref.shape
    shape = total_ref.shape
    place = lax.broadcasted_iota(jnp.int32, shape, 0) * LANES + lax.broadcasted_iota(
        jnp.int32, shape, 1
    )
    mine = jnp.zeros(shape, jnp.float32)
    for i in range(blocks_here):
        wide = grad_ref[i].astype(jnp.float32)
        rows = jnp.sum(wide * wide, axis=0, keepdims=True)
        trace = jnp.sum(rows, axis=1, keepdims=True) * (1.0 / columns)
        mine = jnp.where(place == i * holders + me, trace, mine)
    slots[me] = mine
    pl.semaphore_wait(barrier, holders - 1)
    copies = []
    for peer in peers:
        copy = pltpu.make_async_remote_copy(
            src_ref=slots.at[me],
            dst_ref=slots.at[me],
            send_sem=send_sem.at[peer],
            recv_sem=recv_sem.at[me],
            device_id={"mp": peer},
            device_id_type=pl.DeviceIdType.MESH,
        )
        copy.start()
        copies.append(copy)
    for peer in peers:
        pltpu.make_async_remote_copy(
            src_ref=slots.at[peer],
            dst_ref=slots.at[peer],
            send_sem=send_sem.at[peer],
            recv_sem=recv_sem.at[peer],
            device_id={"mp": peer},
            device_id_type=pl.DeviceIdType.MESH,
        ).wait_recv()
    total = slots[0]
    for i in range(1, holders):
        total = total + slots[i]
    total_ref[...] = total
    for copy in copies:
        copy.wait_send()


def exchange_traces(gradient, holders, blocks):
    rows = -(-blocks // (8 * LANES)) * 8
    return pl.pallas_call(
        functools.partial(trace_exchange, holders),
        out_shape=jax.ShapeDtypeStruct((rows, LANES), jnp.float32),
        in_specs=[pl.BlockSpec(memory_space=pltpu.VMEM)],
        out_specs=pl.BlockSpec(memory_space=pltpu.VMEM),
        scratch_shapes=[
            pltpu.VMEM((holders, rows, LANES), jnp.float32),
            pltpu.SemaphoreType.DMA((holders,)),
            pltpu.SemaphoreType.DMA((holders,)),
        ],
        compiler_params=pltpu.CompilerParams(
            collective_id=0, has_side_effects=True, vmem_limit_bytes=32 * 1024 * 1024
        ),
    )(gradient)


def matmul(left, right):
    return jnp.dot(left, right, preferred_element_type=jnp.float32)


def halves(wide):
    high = wide.astype(jnp.bfloat16)
    return high, (wide - high.astype(jnp.float32)).astype(jnp.bfloat16)


def eye_of(order):
    return jnp.where(
        lax.broadcasted_iota(jnp.int32, (order, order), 0)
        == lax.broadcasted_iota(jnp.int32, (order, order), 1),
        1.0,
        0.0,
    ).astype(jnp.float32)


def total_of(wide):
    return jnp.sum(jnp.sum(wide, axis=0, keepdims=True), axis=1, keepdims=True)


def root_kernel(holders, ids_ref, grad_ref, map_ref, trace_ref, root_ref):
    together, order, columns = grad_ref.shape
    first = pl.program_id(0) * together
    holder = lax.axis_index("mp")
    eye = eye_of(order)
    layers = map_ref[...]
    traces = trace_ref[0 : layers.shape[0], :]
    state = []
    for j in range(together):
        block = (first + j) * holders + holder
        layer = ids_ref[block]
        same = layers == layer
        total = total_of(jnp.where(same, traces, 0.0))
        count = total_of(jnp.where(same, 1.0, 0.0))
        ridge = 0.1 * total / (count * order)
        grad = grad_ref[j]
        stats = lax.dot_general(
            grad, grad, (((1,), (1,)), ((), ())), preferred_element_type=jnp.float32
        ) * (1.0 / columns)
        damped = stats + ridge * eye
        scaled = 2.5 / jnp.sqrt(total_of(damped * damped))
        m = scaled * (total_of(damped * eye) * (1.0 / order))
        h = scaled * damped - m * eye
        state.append((m, h, jnp.sqrt(jnp.sqrt(scaled)), None))
    for k in range(ITERS):
        after = []
        for m, h, x, y in state:
            if k in RECENTRE:
                shift = total_of(h * eye) * (1.0 / order)
                m = m + shift
                h = h - shift * eye
            f = 1.25 - 0.25 * m
            high, low = halves(h)
            if k == 0:
                y = (-0.25 * x) * h
            else:
                y = f * y + (-0.25 * x) * h - 0.25 * matmul(y.astype(jnp.bfloat16), high)
            x = x * f
            if k < ITERS - 1:
                e = (-0.5 * f) * h + 0.0625 * matmul(high, high)
                eb = e.astype(jnp.bfloat16)
                s = f * f
                g = (2.0 * s) * e + matmul(eb, eb)
                t = s * s
                ghigh, glow = halves(g)
                h = (
                    t * h
                    + m * g
                    + (matmul(ghigh, high) + matmul(ghigh, low) + matmul(glow, high))
                )
                m = t * m
            after.append((m, h, x, y))
        state = after
    for j in range(together):
        m, h, x, y = state[j]
        root_ref[j] = y + x * eye


def local_whole(grads, layer_map):
    gradient = grads[0, :, 0]
    blocks_here, order, columns = gradient.shape
    holders = lax.axis_size("mp")
    blocks = blocks_here * holders
    traces = exchange_traces(gradient, holders, blocks)
    together = TOGETHER if blocks_here % TOGETHER == 0 else 1
    padded = -(-blocks // LANES) * LANES
    layers = jnp.pad(layer_map, (0, padded - blocks), constant_values=-1).reshape(-1, LANES)
    roots = pl.pallas_call(
        functools.partial(root_kernel, holders),
        out_shape=jax.ShapeDtypeStruct((blocks_here, order, order), jnp.float32),
        grid_spec=pltpu.PrefetchScalarGridSpec(
            num_scalar_prefetch=1,
            grid=(blocks_here // together,),
            in_specs=[
                pl.BlockSpec((together, order, columns), lambda i, ids: (i, 0, 0)),
                pl.BlockSpec(layers.shape, lambda i, ids: (0, 0)),
                pl.BlockSpec(traces.shape, lambda i, ids: (0, 0)),
            ],
            out_specs=pl.BlockSpec((together, order, order), lambda i, ids: (i, 0, 0)),
        ),
        compiler_params=pltpu.CompilerParams(vmem_limit_bytes=48 * 1024 * 1024),
    )(layer_map, gradient, layers, traces)
    return roots.reshape(blocks_here, 1, order, order)


def local(grads, layer_map):
    if lax.axis_size("dp") == 1:
        return local_whole(grads, layer_map)
    return local_split(grads, layer_map)


def solution(mesh):
    placed = (P("dp", None, "mp", None, None), P())
    return jax.shard_map(
        local, mesh=mesh, in_specs=placed, out_specs=P(None, "mp", "dp", None), check_vma=False
    )
```

profile of v0, /device:TPU:0, one launch (start us, length us, event | category | flops | bytes accessed | tf_op | source)
XLA Modules:
  0.0 66.2 jit_solution(6599977542547317440)
XLA Ops:
  0.0 0.0 copy-start
  0.0 1.6 %copy-done = bf16[1,16,1,256,256]{4,3,2,1,0:T(8,128)(2,1)S(1)} copy-done((bf16[1,16,1,256,256]{4,3,2,1,0:T(8,128)(2,1)S(1)}, bf16[1,16,1,256,256]{4,3,2,1,0:T(8,128)(2,1)}, u32[]{:S(2)}) %copy-start) | copy-done | bytes 2097176
  1.6 10.6 %shard_map.28.trace_ref = f32[8,128]{1,0:T(8,128)S(1)} custom-call(bf16[16,256,256]{2,1,0:T(8,128)(2,1)S(1)} %bitcast.5), custom_call_target="tpu_custom_call" | custom-call | tf_op jit(solution)/shard_map/pallas_call | solution.py:124
  12.2 0.0 copy-start.1
  12.2 1.6 %copy-done.1 = bf16[1,16,1,256,256]{4,3,2,1,0:T(8,128)(2,1)S(1)} copy-done((bf16[1,16,1,256,256]{4,3,2,1,0:T(8,128)(2,1)S(1)}, bf16[1,16,1,256,256]{4,3,2,1,0:T(8,128)(2,1)}, u32[]{:S(2)}) %copy-start.1) | copy-done | bytes 2097176
  13.8 0.0 copy-start.2
  13.8 0.7 %copy-done.2 = s32[512]{0:T(512)S(1)} copy-done((s32[512]{0:T(512)S(1)}, s32[512]{0:T(512)}, u32[]{:S(2)}) %copy-start.2) | copy-done | bytes 2072
  14.4 51.8 %shard_map.29 = f32[16,256,256]{2,1,0:T(8,128)} custom-call(s32[512]{0:T(512)S(1)} %copy-done.2, bf16[16,256,256]{2,1,0:T(8,128)(2,1)S(1)} %bitcast.6, s32[4,128]{1,0:T(4,128)S(1)} %bitcast.7, f32[8,128]{1,0:T(8,128)S(1)} %shard_map.28.trace_ref), custom_call_target="tpu_custom_call" | custom-call | tf_op jit(solution)/shard_map/pallas_call | solution.py:229
Async XLA Ops:
  0.0 1.6 %copy-start = (bf16[1,16,1,256,256]{4,3,2,1,0:T(8,128)(2,1)S(1)}, bf16[1,16,1,256,256]{4,3,2,1,0:T(8,128)(2,1)}, u32[]{:S(2)}) copy-start(bf16[1,16,1,256,256]{4,3,2,1,0:T(8,128)(2,1)} %param.2) | copy-start | bytes 6291460
  12.2 1.6 %copy-start.1 = (bf16[1,16,1,256,256]{4,3,2,1,0:T(8,128)(2,1)S(1)}, bf16[1,16,1,256,256]{4,3,2,1,0:T(8,128)(2,1)}, u32[]{:S(2)}) copy-start(bf16[1,16,1,256,256]{4,3,2,1,0:T(8,128)(2,1)} %param.2) | copy-start | bytes 6291460
  13.8 0.7 %copy-start.2 = (s32[512]{0:T(512)S(1)}, s32[512]{0:T(512)}, u32[]{:S(2)}) copy-start(s32[512]{0:T(512)} %ids_ref.1) | copy-start | bytes 6148
where the time goes:
time: 66.4 us; the launch traced here: 66.2 us
  Pallas kernels  62.3 us (94%)
  local copies, waits for them, and re-layouts  3.86 us (6%)
    pallas_call x1, Pallas kernels, local_whole(): pl.pallas_call(functools.partial(root_kernel, holders), out_shape=jax.Sha...  51.8 us
    pallas_call x1, Pallas kernels, exchange_traces(): pl.pallas_call(functools.partial(trace_exchange, holders), out_shape=jax....  10.6 us
    unnamed x6, local copies, waits for them, and re-layouts  3.86 us

commit v1 on v0

--- a/solution.py
+++ b/solution.py
@@ -65,7 +65,7 @@
 
 
 LANES = 128
-TOGETHER = 2
+TOGETHER = 4
 RECENTRE = (2, 4, 6)
 
 
@@ -166,7 +166,7 @@
     eye = eye_of(order)
     layers = map_ref[...]
     traces = trace_ref[0 : layers.shape[0], :]
-    state = []
+    m, h, x, y = [], [], [], []
     for j in range(together):
         block = (first + j) * holders + holder
         layer = ids_ref[block]
@@ -180,41 +180,48 @@
         ) * (1.0 / columns)
         damped = stats + ridge * eye
         scaled = 2.5 / jnp.sqrt(total_of(damped * damped))
-        m = scaled * (total_of(damped * eye) * (1.0 / order))
-        h = scaled * damped - m * eye
-        state.append((m, h, jnp.sqrt(jnp.sqrt(scaled)), None))
+        m.append(scaled * (total_of(damped * eye) * (1.0 / order)))
+        h.append(scaled * damped - m[j] * eye)
+        x.append(jnp.sqrt(jnp.sqrt(scaled)))
+        y.append(None)
+    every = range(together)
     for k in range(ITERS):
-        after = []
-        for m, h, x, y in state:
-            if k in RECENTRE:
-                shift = total_of(h * eye) * (1.0 / order)
-                m = m + shift
-                h = h - shift * eye
-            f = 1.25 - 0.25 * m
-            high, low = halves(h)
+        last = k == ITERS - 1
+        if k in RECENTRE:
+            for j in every:
+                shift = total_of(h[j] * eye) * (1.0 / order)
+                m[j] = m[j] + shift
+                h[j] = h[j] - shift * eye
+        f = [1.25 - 0.25 * m[j] for j in every]
+        high, low, eb, e, g, ghigh, glow = ([None] * together for _ in range(7))
+        for j in every:
+            high[j], low[j] = halves(h[j])
+            if not last:
+                e[j] = (-0.5 * f[j]) * h[j] + 0.0625 * matmul(high[j], high[j])
+                eb[j] = e[j].astype(jnp.bfloat16)
+        for j in every:
             if k == 0:
-                y = (-0.25 * x) * h
+                y[j] = (-0.25 * x[j]) * h[j]
             else:
-                y = f * y + (-0.25 * x) * h - 0.25 * matmul(y.astype(jnp.bfloat16), high)
-            x = x * f
-            if k < ITERS - 1:
-                e = (-0.5 * f) * h + 0.0625 * matmul(high, high)
-                eb = e.astype(jnp.bfloat16)
-                s = f * f
-                g = (2.0 * s) * e + matmul(eb, eb)
-                t = s * s
-                ghigh, glow = halves(g)
-                h = (
-                    t * h
-                    + m * g
-                    + (matmul(ghigh, high) + matmul(ghigh, low) + matmul(glow, high))
-                )
-                m = t * m
-            after.append((m, h, x, y))
-        state = after
-    for j in range(together):
-        m, h, x, y = state[j]
-        root_ref[j] = y + x * eye
+                yb = y[j].astype(jnp.bfloat16)
+                y[j] = f[j] * y[j] + (-0.25 * x[j]) * h[j] - 0.25 * matmul(yb, high[j])
+            x[j] = x[j] * f[j]
+            if not last:
+                s = f[j] * f[j]
+                g[j] = (2.0 * s) * e[j] + matmul(eb[j], eb[j])
+                ghigh[j], glow[j] = halves(g[j])
+        if last:
+            break
+        for j in every:
+            t = f[j] * f[j] * f[j] * f[j]
+            product = matmul(
+                jnp.concatenate([ghigh[j], ghigh[j], glow[j]], axis=1),
+                jnp.concatenate([high[j], low[j], high[j]], axis=0),
+            )
+            h[j] = t * h[j] + m[j] * g[j] + product
+            m[j] = t * m[j]
+    for j in every:
+        root_ref[j] = y[j] + x[j] * eye
 
 
 def local_whole(grads, layer_map):
@@ -239,7 +246,7 @@
             ],
             out_specs=pl.BlockSpec((together, order, order), lambda i, ids: (i, 0, 0)),
         ),
-        compiler_params=pltpu.CompilerParams(vmem_limit_bytes=48 * 1024 * 1024),
+        compiler_params=pltpu.CompilerParams(vmem_limit_bytes=60 * 1024 * 1024),
     )(layer_map, gradient, layers, traces)
     return roots.reshape(blocks_here, 1, order, order)
 

time: 66.4 us -> 54.2 us (0.82)
  Pallas kernels: 62.3 us -> 51.8 us
  local copies, waits for them, and re-layouts: 3.86 us -> 2.17 us
    pallas_call x1, Pallas kernels: 51.8 us -> 41.2 us  [local_whole(): pl.pallas_call(functools.partial(root_kernel, holders), out_shape=jax.Sha...]
    unnamed x6 -> x4, local copies, waits for them, and re-layouts: 3.86 us -> 2.17 us
where the time goes in v1:
time: 54.2 us; the launch traced here: 54 us
  Pallas kernels  51.8 us (96%)
  local copies, waits for them, and re-layouts  2.17 us (4%)
    pallas_call x1, Pallas kernels, local_whole(): pl.pallas_call(functools.partial(root_kernel, holders), out_shape=jax.Sha...  41.2 us
    pallas_call x1, Pallas kernels, exchange_traces(): pl.pallas_call(functools.partial(trace_exchange, holders), out_shape=jax....  10.6 us
    unnamed x4, local copies, waits for them, and re-layouts  2.17 us

profile of v1, /device:TPU:0, one launch (start us, length us, event | category | flops | bytes accessed | tf_op | source)
XLA Modules:
  0.0 54.0 jit_solution(16662004556741249852)
XLA Ops:
  0.0 0.0 copy-start
  0.0 1.6 %copy-done = bf16[1,16,1,256,256]{4,3,2,1,0:T(8,128)(2,1)S(1)} copy-done((bf16[1,16,1,256,256]{4,3,2,1,0:T(8,128)(2,1)S(1)}, bf16[1,16,1,256,256]{4,3,2,1,0:T(8,128)(2,1)}, u32[]{:S(2)}) %copy-start) | copy-done | bytes 2097176
  1.6 10.6 %shard_map.28.trace_ref = f32[8,128]{1,0:T(8,128)S(1)} custom-call(bf16[16,256,256]{2,1,0:T(8,128)(2,1)S(1)} %bitcast.6), custom_call_target="tpu_custom_call" | custom-call | tf_op jit(solution)/shard_map/pallas_call | solution.py:124
  12.2 0.0 copy-start.1
  12.2 0.6 %copy-done.1 = f32[8,128]{1,0:T(8,128)} copy-done((f32[8,128]{1,0:T(8,128)}, f32[8,128]{1,0:T(8,128)S(1)}, u32[]{:S(2)}) %copy-start.1) | copy-done | bytes 4120
  12.7 41.2 %shard_map.29 = f32[16,256,256]{2,1,0:T(8,128)} custom-call(s32[512]{0:T(512)} %ids_ref.1, bf16[16,256,256]{2,1,0:T(8,128)(2,1)} %bitcast.5, s32[4,128]{1,0:T(4,128)} %bitcast.7, f32[8,128]{1,0:T(8,128)} %copy-done.1), custom_call_target="tpu_custom_call" | custom-call | tf_op jit(solution)/shard_map/pallas_call | solution.py:236
Async XLA Ops:
  0.0 1.6 %copy-start = (bf16[1,16,1,256,256]{4,3,2,1,0:T(8,128)(2,1)S(1)}, bf16[1,16,1,256,256]{4,3,2,1,0:T(8,128)(2,1)}, u32[]{:S(2)}) copy-start(bf16[1,16,1,256,256]{4,3,2,1,0:T(8,128)(2,1)} %param.2) | copy-start | bytes 6291460
  12.2 0.6 %copy-start.1 = (f32[8,128]{1,0:T(8,128)}, f32[8,128]{1,0:T(8,128)S(1)}, u32[]{:S(2)}) copy-start(f32[8,128]{1,0:T(8,128)S(1)} %shard_map.28.trace_ref) | copy-start | bytes 12292
